TPU v7x, 32 devices: a whole 2x2x4 slice. The times are simulated.
32 devices in a mesh: phonon: 2 (over x), beam: 8 (over z, y), sub: 2 (over core).
Axes of the slice: x: 2, y: 2, z: 4, core: 2. Of those that a mesh axis runs over, the one named last changes fastest.
Arguments:
- atom_species: int32 [4, 2048], P('phonon'), parts along dimension 0, may hold values from 0 to 3
- atom_cells: int32 [2, 4, 2048], P(None, 'phonon'), parts along dimension 1, may hold values from 0 to 511
- profiles: bfloat16 [4, 512], replicated, may hold values from -6 to 6
- beam_freqs: int32 [2, 32], P(None, ('beam', 'sub')), may hold values from -32 to 30, as said below
- amplitude: float32 [32], P(('beam', 'sub')), may hold values from 0.5 to 2
- aberration: float32 [32], P(('beam', 'sub')), may hold values from -3.140625 to 3.140625
- probes: int32 [2, 64], replicated, may hold values from 0 to 255
Outputs:
- intensity: float32 [128, 256, 256], P('phonon', ('beam', 'sub')), parts along dimension 0
There are 2 independent parts, one for each index of `phonon`. A program takes and returns all parts, laid end to end along the dimension named above; an argument that names none is the same for every part. Nothing has to cross between parts.
Inputs may be any that keep to these rules, and one draw needn't show every extreme that they name: `beam_freqs`: every column is a pair of even frequencies; no pair repeats.
All inputs are finite; a program needn't handle non-finite values.
Results may differ from a plain program's by a relative error of at most 0.015.
Values may be sent and summed in bfloat16 or wider, within the bound.
A program may use at most 64 MiB of HBM per device.

v0:
```python
import functools
import math

import jax
import jax.numpy as jnp
import ml_dtypes
import numpy as np
from jax import lax
from jax.experimental import pallas as pl
from jax.experimental.pallas import tpu as pltpu
from jax.sharding import PartitionSpec as P

NOUT = 256
LOW = 64
BF = jnp.bfloat16
F32 = jnp.float32


def fit_turn_polys():
    nodes = np.cos(np.pi * (np.arange(400) + 0.5) / 400)
    squares = (nodes + 1.0) * 0.125
    turns = np.sqrt(squares)
    cosine = np.polynomial.chebyshev.Chebyshev.fit(
        squares, np.cos(2 * np.pi * turns), 6, domain=[0, 0.25]
    )
    sine = np.polynomial.chebyshev.Chebyshev.fit(
        squares, np.sin(2 * np.pi * turns) / turns, 6, domain=[0, 0.25]
    )
    to_list = lambda fit: [float(c) for c in fit.convert(kind=np.polynomial.Polynomial).coef]
    return to_list(cosine), to_list(sine)


COS_POLY, SIN_POLY = fit_turn_polys()


def cos_sin_turns(turns):
    rest = turns - jnp.round(turns)
    square = rest * rest
    cosine = jnp.full_like(square, COS_POLY[-1])
    for c in COS_POLY[-2::-1]:
        cosine = cosine * square + c
    sine = jnp.full_like(square, SIN_POLY[-1])
    for c in SIN_POLY[-2::-1]:
        sine = sine * square + c
    return cosine, sine * rest


def window_freqs(points):
    half = NOUT // 2
    reach = math.isqrt((points * points - 1) // 9)
    side = max(reach + 1, half)
    side = min(-(-side // 64) * 64, points // 2)
    return np.concatenate(
        [np.arange(-half, half), np.arange(half, side), np.arange(-side, -half)]
    ).astype(np.int64)


def table_parts(rows, cols, modulus, sign):
    angle = sign * 2.0 * np.pi / modulus * np.mod(rows[:, None] * cols[None, :], modulus)
    return np.cos(angle), np.sin(angle)


def left_table(real, imag):
    return np.block([[real, -imag], [imag, real]]).astype(ml_dtypes.bfloat16)


def right_table(real, imag):
    return np.block([[real, imag], [-imag, real]]).astype(ml_dtypes.bfloat16)


def propagator_parts(freqs, points):
    q = freqs[:, None] ** 2 + freqs[None, :] ** 2
    angle = -np.pi / points * np.mod(q, 2 * points)
    window = np.where(9 * q < points * points, 1.0 / (points * points), 0.0)
    return np.stack([np.cos(angle) * window, np.sin(angle) * window]).astype(np.float32)


def dot(a, b):
    return jnp.dot(a, b, preferred_element_type=F32)


def wave_kernel(
    total_beams,
    freqs_ref,
    amp_ref,
    aber_ref,
    species_ref,
    cells_ref,
    prof_ref,
    probes_ref,
    lf_ref,
    rf_ref,
    lg_ref,
    rg_ref,
    lfc_ref,
    rfc_ref,
    lgc_ref,
    rgc_ref,
    pf_ref,
    out_ref,
    coef_ref,
    field_ref,
    rows_ref,
    tall_ref,
    wide_ref,
    tall_c,
    wide_c,
):
    kinds, points = prof_ref.shape
    slices, atoms = species_ref.shape
    beams = out_ref.shape[0]
    window = pf_ref.shape[1]

    stacked = []
    for s in range(kinds):
        row = jnp.broadcast_to(prof_ref[s : s + 1, :].astype(F32), (LOW, points))
        stacked.append(pltpu.roll(row, 0, 1, stride=1, stride_axis=0))
    tab = jnp.transpose(jnp.concatenate(stacked, axis=0)).astype(BF)

    scale = 1.5 / math.sqrt(atoms) / (2.0 * math.pi)
    chunk = min(512, atoms)
    slot = lax.broadcasted_iota(jnp.int32, (kinds * LOW, chunk), 0)
    for layer in range(slices):
        for axis in range(2):
            for first in range(0, atoms, chunk):
                here = slice(first, first + chunk)
                cell = cells_ref[axis, layer : layer + 1, here]
                key = species_ref[layer : layer + 1, here] * LOW + jnp.bitwise_and(cell, LOW - 1)
                picked = (slot == key).astype(F32).astype(BF)
                rows = dot(tab, picked)
                amount = LOW
                while amount < points:
                    moved = jnp.concatenate([rows[points - amount :], rows[: points - amount]], 0)
                    rows = jnp.where(jnp.bitwise_and(cell, amount) != 0, moved, rows)
                    amount *= 2
                rows_ref[axis, :, here] = rows.astype(BF)
        field = lax.dot_general(
            rows_ref[0], rows_ref[1], (((1,), (1,)), ((), ())), preferred_element_type=F32
        )
        cosine, sine = cos_sin_turns(field * scale)
        field_ref[2 * layer] = cosine
        field_ref[2 * layer + 1] = sine

    down = lax.broadcasted_iota(jnp.int32, (points, 1), 0)
    along = lax.broadcasted_iota(jnp.int32, (1, points), 1)
    for b in range(beams):
        fx, fy = freqs_ref[0, b], freqs_ref[1, b]
        col_re, col_im = cos_sin_turns(
            jnp.bitwise_and(down * fx, points - 1).astype(F32) * (1.0 / points)
        )
        row_re, row_im = cos_sin_turns(
            jnp.bitwise_and(along * fy, points - 1).astype(F32) * (1.0 / points)
        )
        wave_re = col_re * row_re - col_im * row_im
        wave_im = col_re * row_im + col_im * row_re
        for layer in range(slices):
            tr, ti = field_ref[2 * layer], field_ref[2 * layer + 1]
            tall_ref[:points] = (wave_re * tr - wave_im * ti).astype(BF)
            tall_ref[points:] = (wave_re * ti + wave_im * tr).astype(BF)
            last = layer == slices - 1
            n = NOUT if last else window
            lf, rf = (lfc_ref, rfc_ref) if last else (lf_ref, rf_ref)
            lg, rg = (lgc_ref, rgc_ref) if last else (lg_ref, rg_ref)
            width = rg.shape[1] // 2
            wide_ref[:n, :points] = dot(lf[:n], tall_ref[...]).astype(BF)
            wide_ref[:n, points:] = dot(lf[n:], tall_ref[...]).astype(BF)
            half = wide_ref[:n]
            sr = dot(half, rf[:, :n])
            si = dot(half, rf[:, n:])
            pr, pi = pf_ref[0, :n, :n], pf_ref[1, :n, :n]
            tall_c[:n, :n] = (sr * pr - si * pi).astype(BF)
            tall_c[n : 2 * n, :n] = (sr * pi + si * pr).astype(BF)
            shaped = tall_c[: 2 * n, :n]
            wide_c[:width, :n] = dot(lg[:width], shaped).astype(BF)
            wide_c[:width, n : 2 * n] = dot(lg[width:], shaped).astype(BF)
            back = wide_c[:width, : 2 * n]
            wave_re = dot(back, rg[:, :width])
            wave_im = dot(back, rg[:, width:])
        out_ref[b, 0] = wave_re.astype(BF)
        out_ref[b, 1] = wave_im.astype(BF)
        place = probes_ref[0:1, :] * fx + probes_ref[1:2, :] * fy
        turns = jnp.bitwise_and(place, NOUT - 1).astype(F32) * (1.0 / NOUT)
        cosine, sine = cos_sin_turns(turns + aber_ref[b] * (0.5 / math.pi))
        weight = amp_ref[b] * (1.0 / math.sqrt(total_beams))
        coef_ref[b, 0:1, :] = weight * cosine
        coef_ref[b, 1:2, :] = -(weight * sine)


def local_waves(species, cells, profiles, freqs, amplitude, aberration, probes, total_beams):
    points = profiles.shape[1]
    beams = freqs.shape[1]
    atoms = species.shape[1]
    kept = window_freqs(points)
    window = len(kept)
    grid = np.arange(points)
    coarse = np.arange(NOUT)
    crop = kept[:NOUT]
    fr, fi = table_parts(kept, grid, points, -1.0)
    cr, ci = fr[:NOUT], fi[:NOUT]
    gr, gi = table_parts(coarse, crop, NOUT, 1.0)
    tables = [
        left_table(fr, fi),
        right_table(fr.T, fi.T),
        left_table(fr.T, -fi.T),
        right_table(fr, -fi),
        left_table(cr, ci),
        right_table(cr.T, ci.T),
        left_table(gr, gi),
        right_table(gr.T, gi.T),
        propagator_parts(kept, points),
    ]
    vmem = pl.BlockSpec(memory_space=pltpu.VMEM)
    smem = pl.BlockSpec(memory_space=pltpu.SMEM)
    return pl.pallas_call(
        functools.partial(wave_kernel, total_beams),
        out_shape=(
            jax.ShapeDtypeStruct((beams, 2, NOUT, NOUT), BF),
            jax.ShapeDtypeStruct((beams, 2, probes.shape[1]), F32),
        ),
        in_specs=[smem] * 3 + [vmem] * (4 + len(tables)),
        out_specs=(vmem, vmem),
        scratch_shapes=[
            pltpu.VMEM((2 * species.shape[0], points, points), F32),
            pltpu.VMEM((2, points, atoms), BF),
            pltpu.VMEM((2 * points, points), BF),
            pltpu.VMEM((window, 2 * points), BF),
            pltpu.VMEM((2 * window, window), BF),
            pltpu.VMEM((points, 2 * window), BF),
        ],
        compiler_params=pltpu.CompilerParams(vmem_limit_bytes=56 * 1024 * 1024),
    )(freqs, amplitude, aberration, species, cells, profiles, probes, *map(jnp.asarray, tables))


def shards(atom_species, atom_cells, profiles, beam_freqs, amplitude, aberration, probes):
    groups = lax.axis_size("beam") * lax.axis_size("sub")
    beams = beam_freqs.shape[1]
    count = probes.shape[1]
    waves, coefs = local_waves(
        atom_species, atom_cells, profiles, beam_freqs, amplitude, aberration, probes, beams * groups
    )
    rows = NOUT // groups
    waves = waves.reshape(beams, 2, groups, rows, NOUT)
    coefs = jnp.pad(coefs.astype(BF), ((0, 0), (0, 0), (0, NOUT - count)))
    coefs = jnp.broadcast_to(coefs[:, :, None, None, :], (beams, 2, groups, 1, NOUT))
    sent = jnp.concatenate([waves, coefs], axis=3)
    got = lax.all_to_all(sent, ("beam", "sub"), split_axis=2, concat_axis=0, tiled=True)
    got = got[:, :, 0]
    coef = got[:, :, rows, :count]
    coef_re, coef_im = coef[:, 0], coef[:, 1]
    flat = got[:, :, :rows].reshape(beams * groups * 2, rows * NOUT)
    left_re = jnp.stack([coef_re, -coef_im], axis=1).reshape(beams * groups * 2, count)
    left_im = jnp.stack([coef_im, coef_re], axis=1).reshape(beams * groups * 2, count)
    over = (((0,), (0,)), ((), ()))
    psi_re = lax.dot_general(left_re, flat, over, preferred_element_type=F32)
    psi_im = lax.dot_general(left_im, flat, over, preferred_element_type=F32)
    return (psi_re * psi_re + psi_im * psi_im).reshape(count, rows, NOUT)


def solution(mesh):
    return jax.shard_map(
        shards,
        mesh=mesh,
        in_specs=(
            P("phonon", None),
            P(None, "phonon", None),
            P(),
            P(None, ("beam", "sub")),
            P(("beam", "sub")),
            P(("beam", "sub")),
            P(),
        ),
        out_specs=P("phonon", ("beam", "sub"), None),
        check_vma=False,
    )
```

profile of v0, /device:TPU:0, one launch (start us, length us, event | category | flops | bytes accessed | tf_op | source)
XLA Modules:
  0.0 52.1 jit_solution(8093752333439947808)
XLA Ops:
  0.0 22.3 %shard_map.154 = (bf16[2,2,256,256]{3,2,1,0:T(8,128)(2,1)}, f32[2,2,64]{2,1,0:T(2,128)}) custom-call(s32[2,2]{1,0:T(2,128)} %freqs_ref.1, f32[2]{0:T(128)} %amp_ref.1, f32[2]{0:T(128)} %aber_ref.1, s32[2,2048]{1,0:T(2,128)} %species_ref.1, s32[2,2,2048]{2,1,0:T(2,128)} %cells_ref.1, bf16[4,512]{1,0:T(4,128)(2,1)} %prof_ref.1, s32[2,64]{1,0:T(2,128)} %probes_ref.1, ...), custom_call_target="tpu_custom_call" | custom-call | tf_op jit(solution)/shard_map/pallas_call | solution.py:214
  22.3 1.6 %copy.19 = bf16[2,2,16,16,256]{4,1,3,0,2:T(2,128)(2,1)S(1)} copy(bf16[2,2,16,16,256]{4,3,2,1,0:T(8,128)(2,1)} %bitcast.26) | data formatting | bytes 1048576 | tf_op jit(solution)/shard_map/reshape | solution.py:242
  23.9 0.7 %convert_element_type.5 = bf16[2,2,64]{2,1,0:T(2,128)(2,1)S(1)} convert(f32[2,2,64]{2,1,0:T(2,128)} %get-tuple-element.8) | non-fusion elementwise | flops 256 | bytes 1536 | tf_op jit(solution)/shard_map/convert_element_type | solution.py:243
  24.6 0.7 %pad_maximum_fusion = bf16[2,2,16,17,256]{4,1,3,0,2:T(2,128)(2,1)S(1)} fusion(bf16[2,2,16,1,256]{4,1,3,0,2:T(2,128)(2,1)S(1)} %broadcast_in_dim.2, bf16[2,2,16,16,256]{4,1,3,0,2:T(2,128)(2,1)S(1)} %copy.19), kind=kLoop, calls=%fused_computation.3 | loop fusion | flops 278528 | bytes 1114112 | tf_op jit(solution)/shard_map/concatenate | solution.py:245
  25.3 23.9 %all_to_all.15 = bf16[2,2,16,17,256]{4,1,3,0,2:T(2,128)(2,1)S(1)} all-to-all(bf16[2,2,16,17,256]{4,1,3,0,2:T(2,128)(2,1)S(1)} %pad_maximum_fusion), channel_id=1, replica_groups=mesh['phonon'=2,'beam'=8,'sub'=2] {'beam','sub'}, dimensions={2} | all-to-all | bytes 1114112 | tf_op jit(solution)/shard_map/all_to_all | solution.py:246
  49.3 0.5 %slice.19 = bf16[32,2,16,256]{3,1,2,0:T(2,128)(2,1)S(1)} slice(bf16[32,2,17,256]{3,1,2,0:T(2,128)(2,1)S(1)} %bitcast.24), slice={[0:32], [0:2], [0:16], [0:256]} | slice | bytes 1048576 | tf_op jit(solution)/shard_map/slice | solution.py:250
  49.8 0.1 copy.22
  49.9 0.2 copy.24
  50.2 0.3 convolution_multiply_fusion
  50.5 0.3 fusion
  50.8 1.3 %copy.25 = f32[8,8,16,256]{3,2,1,0:T(8,128)} copy(f32[8,8,16,256]{3,1,2,0:T(8,128)S(1)} %bitcast.22) | data formatting | bytes 2097152
  (8 shorter events, 0.1 us)
where the time goes:
time: 52.3 us; the launch traced here: 52.1 us
  blocking collectives  23.9 us (46%)
  Pallas kernels  22.3 us (43%)
  local copies, waits for them, and re-layouts  3.76 us (7%)
  other arithmetic  1.41 us (3%)
  matrix products  0.64 us (1%)
    all_to_all x1, blocking collectives, shards(): lax.all_to_all(sent, ('beam', 'sub'), split_axis=2, concat_axis=0, tiled=...  23.9 us
    pallas_call x1, Pallas kernels, local_waves(): pl.pallas_call(functools.partial(wave_kernel, total_beams), out_shape=(ja...  22.3 us
    reshape x1, local copies, waits for them, and re-layouts, shards(): waves = waves.reshape(beams, 2, groups, rows, NOUT)  1.58 us
    unnamed x2, local copies, waits for them, and re-layouts  1.47 us

commit v1 on v0

--- a/solution.py
+++ b/solution.py
@@ -90,15 +90,10 @@
     probes_ref,
     lf_ref,
     rf_ref,
-    lg_ref,
-    rg_ref,
-    lfc_ref,
-    rfc_ref,
     lgc_ref,
     rgc_ref,
     pf_ref,
     out_ref,
-    coef_ref,
     field_ref,
     rows_ref,
     tall_ref,
@@ -108,7 +103,9 @@
 ):
     kinds, points = prof_ref.shape
     slices, atoms = species_ref.shape
-    beams = out_ref.shape[0]
+    beams = freqs_ref.shape[1]
+    groups = out_ref.shape[0]
+    size = NOUT // groups
     window = pf_ref.shape[1]
 
     stacked = []
@@ -143,6 +140,7 @@
 
     down = lax.broadcasted_iota(jnp.int32, (points, 1), 0)
     along = lax.broadcasted_iota(jnp.int32, (1, points), 1)
+    coef_rows = []
     for b in range(beams):
         fx, fy = freqs_ref[0, b], freqs_ref[1, b]
         col_re, col_im = cos_sin_turns(
@@ -159,14 +157,13 @@
             tall_ref[points:] = (wave_re * ti + wave_im * tr).astype(BF)
             last = layer == slices - 1
             n = NOUT if last else window
-            lf, rf = (lfc_ref, rfc_ref) if last else (lf_ref, rf_ref)
-            lg, rg = (lgc_ref, rgc_ref) if last else (lg_ref, rg_ref)
+            lg, rg = (lgc_ref, rgc_ref) if last else (rf_ref, lf_ref)
             width = rg.shape[1] // 2
-            wide_ref[:n, :points] = dot(lf[:n], tall_ref[...]).astype(BF)
-            wide_ref[:n, points:] = dot(lf[n:], tall_ref[...]).astype(BF)
+            wide_ref[:n, :points] = dot(lf_ref[:n], tall_ref[...]).astype(BF)
+            wide_ref[:n, points:] = dot(lf_ref[window : window + n], tall_ref[...]).astype(BF)
             half = wide_ref[:n]
-            sr = dot(half, rf[:, :n])
-            si = dot(half, rf[:, n:])
+            sr = dot(half, rf_ref[:, :n])
+            si = dot(half, rf_ref[:, window : window + n])
             pr, pi = pf_ref[0, :n, :n], pf_ref[1, :n, :n]
             tall_c[:n, :n] = (sr * pr - si * pi).astype(BF)
             tall_c[n : 2 * n, :n] = (sr * pi + si * pr).astype(BF)
@@ -176,17 +173,87 @@
             back = wide_c[:width, : 2 * n]
             wave_re = dot(back, rg[:, :width])
             wave_im = dot(back, rg[:, width:])
-        out_ref[b, 0] = wave_re.astype(BF)
-        out_ref[b, 1] = wave_im.astype(BF)
+        for part, wave in enumerate((wave_re, wave_im)):
+            start = (2 * b + part) * size
+            if size % 16 == 0:
+                for g in range(groups):
+                    out_ref[g, start : start + size] = wave[g * size : (g + 1) * size].astype(BF)
+            else:
+                blocks = wave.reshape(groups, size, NOUT).astype(BF)
+                out_ref[:, start : start + size] = blocks
         place = probes_ref[0:1, :] * fx + probes_ref[1:2, :] * fy
         turns = jnp.bitwise_and(place, NOUT - 1).astype(F32) * (1.0 / NOUT)
         cosine, sine = cos_sin_turns(turns + aber_ref[b] * (0.5 / math.pi))
         weight = amp_ref[b] * (1.0 / math.sqrt(total_beams))
-        coef_ref[b, 0:1, :] = weight * cosine
-        coef_ref[b, 1:2, :] = -(weight * sine)
-
-
-def local_waves(species, cells, profiles, freqs, amplitude, aberration, probes, total_beams):
+        coef_rows += [weight * cosine, -(weight * sine)]
+    count = probes_ref.shape[1]
+    coefs = jnp.concatenate(coef_rows, axis=0)
+    coefs = jnp.pad(coefs, ((0, 16 - 2 * beams), (0, NOUT - count))).astype(BF)
+    for g in range(groups):
+        out_ref[g, 2 * beams * size :] = coefs
+
+
+def exchange_kernel(groups, sub_size, sent_ref, got_ref, send_sem, recv_sem, own_sem):
+    phonon = lax.axis_index("phonon")
+    me = lax.axis_index("beam") * sub_size + lax.axis_index("sub")
+
+    def device(step):
+        other = lax.rem(me + step, groups)
+        return other, (phonon, lax.div(other, sub_size), lax.rem(other, sub_size))
+
+    barrier = pltpu.get_barrier_semaphore()
+
+    @pl.loop(1, groups)
+    def _(step):
+        pl.semaphore_signal(
+            barrier, inc=1, device_id=device(step)[1], device_id_type=pl.DeviceIdType.MESH
+        )
+
+    own = pltpu.make_async_copy(sent_ref.at[me], got_ref.at[me], own_sem)
+    own.start()
+    pl.semaphore_wait(barrier, groups - 1)
+
+    def copy(step):
+        other, place = device(step)
+        return pltpu.make_async_remote_copy(
+            src_ref=sent_ref.at[other],
+            dst_ref=got_ref.at[me],
+            send_sem=send_sem.at[step],
+            recv_sem=recv_sem.at[step],
+            device_id=place,
+            device_id_type=pl.DeviceIdType.MESH,
+        )
+
+    @pl.loop(1, groups)
+    def _(step):
+        copy(step).start()
+
+    own.wait()
+
+    @pl.loop(1, groups)
+    def _(step):
+        copy(step).wait()
+
+
+def exchange(sent, groups, sub_size):
+    vmem = pl.BlockSpec(memory_space=pltpu.VMEM)
+    return pl.pallas_call(
+        functools.partial(exchange_kernel, groups, sub_size),
+        out_shape=jax.ShapeDtypeStruct(sent.shape, sent.dtype),
+        in_specs=[vmem],
+        out_specs=vmem,
+        scratch_shapes=[
+            pltpu.SemaphoreType.DMA((groups,)),
+            pltpu.SemaphoreType.DMA((groups,)),
+            pltpu.SemaphoreType.DMA,
+        ],
+        compiler_params=pltpu.CompilerParams(
+            collective_id=0, has_side_effects=True, vmem_limit_bytes=16 * 1024 * 1024
+        ),
+    )(sent)
+
+
+def local_waves(species, cells, profiles, freqs, amplitude, aberration, probes, groups):
     points = profiles.shape[1]
     beams = freqs.shape[1]
     atoms = species.shape[1]
@@ -196,15 +263,10 @@
     coarse = np.arange(NOUT)
     crop = kept[:NOUT]
     fr, fi = table_parts(kept, grid, points, -1.0)
-    cr, ci = fr[:NOUT], fi[:NOUT]
     gr, gi = table_parts(coarse, crop, NOUT, 1.0)
     tables = [
         left_table(fr, fi),
         right_table(fr.T, fi.T),
-        left_table(fr.T, -fi.T),
-        right_table(fr, -fi),
-        left_table(cr, ci),
-        right_table(cr.T, ci.T),
         left_table(gr, gi),
         right_table(gr.T, gi.T),
         propagator_parts(kept, points),
@@ -212,13 +274,10 @@
     vmem = pl.BlockSpec(memory_space=pltpu.VMEM)
     smem = pl.BlockSpec(memory_space=pltpu.SMEM)
     return pl.pallas_call(
-        functools.partial(wave_kernel, total_beams),
-        out_shape=(
-            jax.ShapeDtypeStruct((beams, 2, NOUT, NOUT), BF),
-            jax.ShapeDtypeStruct((beams, 2, probes.shape[1]), F32),
-        ),
+        functools.partial(wave_kernel, beams * groups),
+        out_shape=jax.ShapeDtypeStruct((groups, 2 * beams * (NOUT // groups) + 16, NOUT), BF),
         in_specs=[smem] * 3 + [vmem] * (4 + len(tables)),
-        out_specs=(vmem, vmem),
+        out_specs=vmem,
         scratch_shapes=[
             pltpu.VMEM((2 * species.shape[0], points, points), F32),
             pltpu.VMEM((2, points, atoms), BF),
@@ -235,21 +294,17 @@
     groups = lax.axis_size("beam") * lax.axis_size("sub")
     beams = beam_freqs.shape[1]
     count = probes.shape[1]
-    waves, coefs = local_waves(
-        atom_species, atom_cells, profiles, beam_freqs, amplitude, aberration, probes, beams * groups
+    sent = local_waves(
+        atom_species, atom_cells, profiles, beam_freqs, amplitude, aberration, probes, groups
     )
+    got = exchange(sent, groups, lax.axis_size("sub"))
     rows = NOUT // groups
-    waves = waves.reshape(beams, 2, groups, rows, NOUT)
-    coefs = jnp.pad(coefs.astype(BF), ((0, 0), (0, 0), (0, NOUT - count)))
-    coefs = jnp.broadcast_to(coefs[:, :, None, None, :], (beams, 2, groups, 1, NOUT))
-    sent = jnp.concatenate([waves, coefs], axis=3)
-    got = lax.all_to_all(sent, ("beam", "sub"), split_axis=2, concat_axis=0, tiled=True)
-    got = got[:, :, 0]
-    coef = got[:, :, rows, :count]
+    pairs = beams * groups * 2
+    coef = got[:, 2 * beams * rows :, :count][:, : 2 * beams].reshape(-1, 2, count)
     coef_re, coef_im = coef[:, 0], coef[:, 1]
-    flat = got[:, :, :rows].reshape(beams * groups * 2, rows * NOUT)
-    left_re = jnp.stack([coef_re, -coef_im], axis=1).reshape(beams * groups * 2, count)
-    left_im = jnp.stack([coef_im, coef_re], axis=1).reshape(beams * groups * 2, count)
+    flat = got[:, : 2 * beams * rows].reshape(pairs, rows * NOUT)
+    left_re = jnp.stack([coef_re, -coef_im], axis=1).reshape(pairs, count)
+    left_im = jnp.stack([coef_im, coef_re], axis=1).reshape(pairs, count)
     over = (((0,), (0,)), ((), ()))
     psi_re = lax.dot_general(left_re, flat, over, preferred_element_type=F32)
     psi_im = lax.dot_general(left_im, flat, over, preferred_element_type=F32)

time: 52.3 us -> 43.9 us (0.84)
  the two profiles are of different devices: /device:TPU:0 before, /device:TPU:13 now
where the time goes in v1:
time: 43.9 us; the launch traced here: 43.8 us
  Pallas kernels  40.3 us (92%)
  local copies, waits for them, and re-layouts  2.67 us (6%)
  matrix products  0.64 us (1%)
    pallas_call x1, Pallas kernels, local_waves(): pl.pallas_call(functools.partial(wave_kernel, beams * groups), out_shape=...  20.9 us
    pallas_call x1, Pallas kernels, exchange(): pl.pallas_call(functools.partial(exchange_kernel, groups, sub_size), out_...  19.4 us
    unnamed x3, local copies, waits for them, and re-layouts  2.37 us

profile of v1, /device:TPU:13, one launch (start us, length us, event | category | flops | bytes accessed | tf_op | source)
XLA Modules:
  0.0 43.8 jit_solution(16927557276123681458)
XLA Ops:
  0.0 20.9 %shard_map.118.sent_ref = bf16[16,80,256]{2,1,0:T(8,128)(2,1)} custom-call(s32[2,2]{1,0:T(2,128)} %freqs_ref.1, f32[2]{0:T(128)} %amp_ref.1, f32[2]{0:T(128)} %aber_ref.1, s32[2,2048]{1,0:T(2,128)} %species_ref.1, s32[2,2,2048]{2,1,0:T(2,128)} %cells_ref.1, bf16[4,512]{1,0:T(4,128)(2,1)} %prof_ref.1, s32[2,64]{1,0:T(2,128)} %probes_ref.1, ...), custom_call_target="tpu_custom_call" | custom-call | tf_op jit(solution)/shard_map/pallas_call | solution.py:276
  20.9 0.0 copy-start
  20.9 1.1 %copy-done = bf16[16,80,256]{2,1,0:T(8,128)(2,1)S(1)} copy-done((bf16[16,80,256]{2,1,0:T(8,128)(2,1)S(1)}, bf16[16,80,256]{2,1,0:T(8,128)(2,1)}, u32[]{:S(2)}) %copy-start) | copy-done | bytes 655384
  22.0 19.4 %shard_map.119 = bf16[16,80,256]{2,1,0:T(8,128)(2,1)S(1)} custom-call(bf16[16,80,256]{2,1,0:T(8,128)(2,1)S(1)} %copy-done), custom_call_target="tpu_custom_call" | custom-call | tf_op jit(solution)/shard_map/pallas_call | solution.py:240
  41.4 0.2 reshape.17
  41.8 0.1 pad_maximum_fusion
  41.9 0.3 convolution_multiply_fusion
  42.2 0.3 fusion
  42.5 1.3 %copy.13 = f32[8,8,16,256]{3,2,1,0:T(8,128)} copy(f32[8,8,16,256]{3,1,2,0:T(8,128)S(1)} %bitcast.9) | data formatting | bytes 2097152
  (3 shorter events, 0.1 us)
Async XLA Ops:
  20.9 1.1 %copy-start = (bf16[16,80,256]{2,1,0:T(8,128)(2,1)S(1)}, bf16[16,80,256]{2,1,0:T(8,128)(2,1)}, u32[]{:S(2)}) copy-start(bf16[16,80,256]{2,1,0:T(8,128)(2,1)} %shard_map.118.sent_ref) | copy-start | bytes 1966084

commit v2 on v1

--- a/solution.py
+++ b/solution.py
@@ -124,13 +124,14 @@
                 cell = cells_ref[axis, layer : layer + 1, here]
                 key = species_ref[layer : layer + 1, here] * LOW + jnp.bitwise_and(cell, LOW - 1)
                 picked = (slot == key).astype(F32).astype(BF)
-                rows = dot(tab, picked)
+                rows = dot(tab, picked).astype(BF)
                 amount = LOW
                 while amount < points:
                     moved = jnp.concatenate([rows[points - amount :], rows[: points - amount]], 0)
-                    rows = jnp.where(jnp.bitwise_and(cell, amount) != 0, moved, rows)
+                    bit = (jnp.bitwise_and(cell, amount) != 0).astype(F32).astype(BF)
+                    rows = jnp.where(jnp.broadcast_to(bit, rows.shape) > 0.5, moved, rows)
                     amount *= 2
-                rows_ref[axis, :, here] = rows.astype(BF)
+                rows_ref[axis, :, here] = rows
         field = lax.dot_general(
             rows_ref[0], rows_ref[1], (((1,), (1,)), ((), ())), preferred_element_type=F32
         )
@@ -236,12 +237,12 @@
 
 
 def exchange(sent, groups, sub_size):
-    vmem = pl.BlockSpec(memory_space=pltpu.VMEM)
+    place = pl.BlockSpec(memory_space=pl.ANY)
     return pl.pallas_call(
         functools.partial(exchange_kernel, groups, sub_size),
         out_shape=jax.ShapeDtypeStruct(sent.shape, sent.dtype),
-        in_specs=[vmem],
-        out_specs=vmem,
+        in_specs=[place],
+        out_specs=place,
         scratch_shapes=[
             pltpu.SemaphoreType.DMA((groups,)),
             pltpu.SemaphoreType.DMA((groups,)),

time: 43.9 us -> 42.9 us (0.977)
  Pallas kernels: 40.3 us -> 39.3 us
    pallas_call x1, Pallas kernels: 20.9 us -> 19.9 us  [local_waves(): pl.pallas_call(functools.partial(wave_kernel, beams * groups), out_shape=...]
where the time goes in v2:
time: 42.9 us; the launch traced here: 42.8 us
  Pallas kernels  39.3 us (92%)
  local copies, waits for them, and re-layouts  2.67 us (6%)
  matrix products  0.64 us (1%)
    pallas_call x1, Pallas kernels, local_waves(): pl.pallas_call(functools.partial(wave_kernel, beams * groups), out_shape=...  19.9 us
    pallas_call x1, Pallas kernels, exchange(): pl.pallas_call(functools.partial(exchange_kernel, groups, sub_size), out_...  19.4 us
    unnamed x3, local copies, waits for them, and re-layouts  2.37 us

profile of v2, /device:TPU:13, one launch (start us, length us, event | category | flops | bytes accessed | tf_op | source)
XLA Modules:
  0.0 42.8 jit_solution(10738231696474089139)
XLA Ops:
  0.0 19.9 %shard_map.118.sent_ref = bf16[16,80,256]{2,1,0:T(8,128)(2,1)} custom-call(s32[2,2]{1,0:T(2,128)} %freqs_ref.1, f32[2]{0:T(128)} %amp_ref.1, f32[2]{0:T(128)} %aber_ref.1, s32[2,2048]{1,0:T(2,128)} %species_ref.1, s32[2,2,2048]{2,1,0:T(2,128)} %cells_ref.1, bf16[4,512]{1,0:T(4,128)(2,1)} %prof_ref.1, s32[2,64]{1,0:T(2,128)} %probes_ref.1, ...), custom_call_target="tpu_custom_call" | custom-call | tf_op jit(solution)/shard_map/pallas_call | solution.py:277
  19.9 0.0 copy-start
  19.9 1.1 %copy-done = bf16[16,80,256]{2,1,0:T(8,128)(2,1)S(1)} copy-done((bf16[16,80,256]{2,1,0:T(8,128)(2,1)S(1)}, bf16[16,80,256]{2,1,0:T(8,128)(2,1)}, u32[]{:S(2)}) %copy-start) | copy-done | bytes 655384
  20.9 19.4 %shard_map.119 = bf16[16,80,256]{2,1,0:T(8,128)(2,1)S(1)} custom-call(bf16[16,80,256]{2,1,0:T(8,128)(2,1)S(1)} %copy-done), custom_call_target="tpu_custom_call" | custom-call | tf_op jit(solution)/shard_map/pallas_call | solution.py:241
  40.4 0.2 reshape.17
  40.8 0.1 pad_maximum_fusion
  40.9 0.3 convolution_multiply_fusion
  41.2 0.3 fusion
  41.5 1.3 %copy.13 = f32[8,8,16,256]{3,2,1,0:T(8,128)} copy(f32[8,8,16,256]{3,1,2,0:T(8,128)S(1)} %bitcast.9) | data formatting | bytes 2097152
  (3 shorter events, 0.1 us)
Async XLA Ops:
  19.9 1.1 %copy-start = (bf16[16,80,256]{2,1,0:T(8,128)(2,1)S(1)}, bf16[16,80,256]{2,1,0:T(8,128)(2,1)}, u32[]{:S(2)}) copy-start(bf16[16,80,256]{2,1,0:T(8,128)(2,1)} %shard_map.118.sent_ref) | copy-start | bytes 1966084

commit v3 on v2

--- a/solution.py
+++ b/solution.py
@@ -194,7 +194,7 @@
         out_ref[g, 2 * beams * size :] = coefs
 
 
-def exchange_kernel(groups, sub_size, sent_ref, got_ref, send_sem, recv_sem, own_sem):
+def exchange_kernel(groups, sub_size, main, lanes, sent_ref, got_ref, send_sem, recv_sem, own_sem):
     phonon = lax.axis_index("phonon")
     me = lax.axis_index("beam") * sub_size + lax.axis_index("sub")
 
@@ -214,38 +214,46 @@
     own.start()
     pl.semaphore_wait(barrier, groups - 1)
 
-    def copy(step):
+    def copies(turn):
+        step = lax.rem(turn - 1 + groups // 4, groups - 1) + 1
         other, place = device(step)
-        return pltpu.make_async_remote_copy(
-            src_ref=sent_ref.at[other],
-            dst_ref=got_ref.at[me],
-            send_sem=send_sem.at[step],
-            recv_sem=recv_sem.at[step],
-            device_id=place,
-            device_id_type=pl.DeviceIdType.MESH,
-        )
+        pieces = ((pl.ds(0, main), pl.ds(0, NOUT)), (pl.ds(main, 16), pl.ds(0, lanes)))
+        return [
+            pltpu.make_async_remote_copy(
+                src_ref=sent_ref.at[other, rows, cols],
+                dst_ref=got_ref.at[me, rows, cols],
+                send_sem=send_sem.at[k, step],
+                recv_sem=recv_sem.at[k, step],
+                device_id=place,
+                device_id_type=pl.DeviceIdType.MESH,
+            )
+            for k, (rows, cols) in enumerate(pieces)
+        ]
 
     @pl.loop(1, groups)
-    def _(step):
-        copy(step).start()
+    def _(turn):
+        for copy in copies(turn):
+            copy.start()
 
     own.wait()
 
     @pl.loop(1, groups)
-    def _(step):
-        copy(step).wait()
-
-
-def exchange(sent, groups, sub_size):
+    def _(turn):
+        for copy in copies(turn):
+            copy.wait()
+
+
+def exchange(sent, groups, sub_size, count):
+    lanes = min(-(-count // 128) * 128, NOUT)
     place = pl.BlockSpec(memory_space=pl.ANY)
     return pl.pallas_call(
-        functools.partial(exchange_kernel, groups, sub_size),
+        functools.partial(exchange_kernel, groups, sub_size, sent.shape[1] - 16, lanes),
         out_shape=jax.ShapeDtypeStruct(sent.shape, sent.dtype),
         in_specs=[place],
         out_specs=place,
         scratch_shapes=[
-            pltpu.SemaphoreType.DMA((groups,)),
-            pltpu.SemaphoreType.DMA((groups,)),
+            pltpu.SemaphoreType.DMA((2, groups)),
+            pltpu.SemaphoreType.DMA((2, groups)),
             pltpu.SemaphoreType.DMA,
         ],
         compiler_params=pltpu.CompilerParams(
@@ -298,7 +306,7 @@
     sent = local_waves(
         atom_species, atom_cells, profiles, beam_freqs, amplitude, aberration, probes, groups
     )
-    got = exchange(sent, groups, lax.axis_size("sub"))
+    got = exchange(sent, groups, lax.axis_size("sub"), count)
     rows = NOUT // groups
     pairs = beams * groups * 2
     coef = got[:, 2 * beams * rows :, :count][:, : 2 * beams].reshape(-1, 2, count)

time: 42.9 us -> 41.8 us (0.974)
  Pallas kernels: 39.3 us -> 38.1 us
    pallas_call x1, Pallas kernels: 19.4 us -> 18.3 us  [exchange(): pl.pallas_call(functools.partial(exchange_kernel, groups, sub_size, sent....]
where the time goes in v3:
time: 41.8 us; the launch traced here: 41.7 us
  Pallas kernels  38.1 us (91%)
  local copies, waits for them, and re-layouts  2.67 us (6%)
  matrix products  0.65 us (2%)
    pallas_call x1, Pallas kernels, local_waves(): pl.pallas_call(functools.partial(wave_kernel, beams * groups), out_shape=...  19.9 us
    pallas_call x1, Pallas kernels, exchange(): pl.pallas_call(functools.partial(exchange_kernel, groups, sub_size, sent....  18.3 us
    unnamed x3, local copies, waits for them, and re-layouts  2.37 us

profile of v3, /device:TPU:13, one launch (start us, length us, event | category | flops | bytes accessed | tf_op | source)
XLA Modules:
  0.0 41.7 jit_solution(603822506646676121)
XLA Ops:
  0.0 19.9 %shard_map.118.sent_ref = bf16[16,80,256]{2,1,0:T(8,128)(2,1)} custom-call(s32[2,2]{1,0:T(2,128)} %freqs_ref.1, f32[2]{0:T(128)} %amp_ref.1, f32[2]{0:T(128)} %aber_ref.1, s32[2,2048]{1,0:T(2,128)} %species_ref.1, s32[2,2,2048]{2,1,0:T(2,128)} %cells_ref.1, bf16[4,512]{1,0:T(4,128)(2,1)} %prof_ref.1, s32[2,64]{1,0:T(2,128)} %probes_ref.1, ...), custom_call_target="tpu_custom_call" | custom-call | tf_op jit(solution)/shard_map/pallas_call | solution.py:285
  19.9 0.0 copy-start
  19.9 1.1 %copy-done = bf16[16,80,256]{2,1,0:T(8,128)(2,1)S(1)} copy-done((bf16[16,80,256]{2,1,0:T(8,128)(2,1)S(1)}, bf16[16,80,256]{2,1,0:T(8,128)(2,1)}, u32[]{:S(2)}) %copy-start) | copy-done | bytes 655384
  20.9 18.3 %shard_map.119 = bf16[16,80,256]{2,1,0:T(8,128)(2,1)S(1)} custom-call(bf16[16,80,256]{2,1,0:T(8,128)(2,1)S(1)} %copy-done), custom_call_target="tpu_custom_call" | custom-call | tf_op jit(solution)/shard_map/pallas_call | solution.py:249
  39.3 0.2 reshape.17
  39.6 0.1 pad_maximum_fusion
  39.7 0.3 convolution_multiply_fusion
  40.0 0.3 fusion
  40.4 1.3 %copy.13 = f32[8,8,16,256]{3,2,1,0:T(8,128)} copy(f32[8,8,16,256]{3,1,2,0:T(8,128)S(1)} %bitcast.9) | data formatting | bytes 2097152
  (3 shorter events, 0.1 us)
Async XLA Ops:
  19.9 1.1 %copy-start = (bf16[16,80,256]{2,1,0:T(8,128)(2,1)S(1)}, bf16[16,80,256]{2,1,0:T(8,128)(2,1)}, u32[]{:S(2)}) copy-start(bf16[16,80,256]{2,1,0:T(8,128)(2,1)} %shard_map.118.sent_ref) | copy-start | bytes 1966084
